TPU v7x, 512 devices: a whole 4x4x16 slice. The times are simulated.
512 devices in a mesh: seq: 128 (over z, x, core), head: 4 (over y).
Axes of the slice: x: 4, y: 4, z: 16, core: 2. Of those that a mesh axis runs over, the one named last changes fastest.
Arguments:
- queries: bfloat16 [32768, 4096], P('seq', 'head'), may hold values from -100 to 100
- keys_values: bfloat16 [32768, 2, 512], P('seq', None, 'head'), may hold values from -4.5 to 4.5
- cache_kv: bfloat16 [32768, 2, 512], P('seq', None, 'head'), may hold values from -4 to 4
- vertical_pages: int32 [4, 4], P('head'), may hold values from 0 to 255, as said below
- slash_shift: int32 [4, 3], P('head'), may hold values from 1 to 128, as said below
- slash_live: int32 [128, 4, 3], P('seq', 'head'), may hold values 0 or 1
- out_proj: bfloat16 [4096, 2048], P('head'), may hold values from -0.09375 to 0.09375
Outputs:
- projected: bfloat16 [32768, 2048], P('seq', 'head')
Inputs may be any that keep to these rules, and one draw needn't show every extreme that they name: `vertical_pages`: each head group lists 4 distinct pages. `slash_shift`: each head group lists 3 distinct distances.
All inputs are finite; a program needn't handle non-finite values. No bound on the sum of `slash_live` on one device may be relied on, other than what follows from the above.
Results may differ from a plain program's by a relative error of at most 0.0057.
Values may be sent and summed in bfloat16 or wider, within the bound.
A program may use at most 64 MiB of HBM per device.

v0:
```python
import jax
import jax.numpy as jnp
from jax import lax
from jax.sharding import PartitionSpec as P

PAGE = 128


def passed_along(value, axis, steps):
    count = lax.axis_size(axis)
    pairs = [(source, (source + steps) % count) for source in range(count)]
    return lax.ppermute(value, axis, pairs)


def broadcast(value, axis, source):
    kept = jnp.where(lax.axis_index(axis) == source, value, 0).astype(value.dtype)
    return lax.psum(kept, axis)


def rotate(stacked, amounts, shards):
    reduced = amounts % shards
    for bit_number in range(max(1, (shards - 1).bit_length())):
        moved = passed_along(stacked, "seq", 1 << bit_number)
        chosen = reduced // (1 << bit_number) % 2 == 1
        stacked = jnp.where(chosen[:, None, None, None], moved, stacked)
    return stacked


def body(queries, keys_values, cache_kv, vertical_pages, slash_shift, slash_live, out_proj):
    row_count = queries.shape[0]
    head_width = keys_values.shape[2]
    group_heads = queries.shape[1] // head_width
    shards = lax.axis_size("seq")
    own_shard = lax.axis_index("seq")
    distances = slash_shift[0]
    live_blocks = slash_live[0, 0] == 1
    page_ids = vertical_pages[0]
    slash_count = distances.shape[0]
    payload = jnp.where(
        (own_shard < shards - distances)[:, None, None, None], keys_values[None], cache_kv[None]
    )
    slash_kv = jnp.concatenate(
        [
            rotate(payload[position : position + 1], distances[position : position + 1], shards)
            for position in range(slash_count)
        ],
        0,
    )
    per_shard = row_count // PAGE
    owners = page_ids // per_shard
    offsets = page_ids % per_shard * PAGE
    copies = []
    for position in range(page_ids.shape[0]):
        own_page = lax.dynamic_slice_in_dim(cache_kv, offsets[position], PAGE, 0)
        copies.append(broadcast(own_page, "seq", owners[position]))
    vertical = jnp.stack(copies, 0)
    cached_slash = own_shard + shards - distances
    clash = (
        live_blocks[None, :]
        & (distances[None, :] > own_shard)
        & (owners[:, None] == cached_slash[None, :])
    )
    page_open = jnp.logical_not(jnp.any(clash, axis=1))
    row_ids = lax.broadcasted_iota(jnp.int32, (row_count, row_count), 0)
    col_ids = lax.broadcasted_iota(jnp.int32, (row_count, row_count), 1)
    causal = row_ids >= col_ids
    column_open = jnp.concatenate([jnp.repeat(live_blocks, row_count), jnp.repeat(page_open, PAGE)])
    visible = jnp.concatenate(
        [causal, jnp.broadcast_to(column_open[None, :], (row_count, column_open.shape[0]))], 1
    )
    all_keys = jnp.concatenate(
        [keys_values, slash_kv.reshape(-1, 2, head_width), vertical.reshape(-1, 2, head_width)], 0
    )
    query_heads = queries.reshape(row_count, group_heads, head_width)
    scores = jnp.einsum(
        "rgd,kd->grk", query_heads, all_keys[:, 0, :], preferred_element_type=jnp.float32
    )
    scores = scores * head_width ** (-0.5)
    scores = jnp.where(visible[None], scores, -jnp.inf)
    row_max = jnp.max(scores, axis=2, keepdims=True)
    weights = jnp.exp(scores - row_max)
    row_total = jnp.sum(weights, axis=2, keepdims=True)
    weights_bf = (weights / row_total).astype(jnp.bfloat16)
    attended = jnp.einsum(
        "grk,kd->rgd", weights_bf, all_keys[:, 1, :], preferred_element_type=jnp.float32
    )
    attended = attended.astype(jnp.bfloat16).reshape(row_count, group_heads * head_width)
    group_terms = jnp.dot(attended, out_proj, preferred_element_type=jnp.float32)
    return lax.psum_scatter(group_terms, "head", scatter_dimension=1, tiled=True).astype(
        jnp.bfloat16
    )


def solution(mesh):
    placed = (
        P("seq", "head"),
        P("seq", None, "head"),
        P("seq", None, "head"),
        P("head", None),
        P("head", None),
        P("seq", "head", None),
        P("head", None),
    )
    return jax.shard_map(
        body, mesh=mesh, in_specs=placed, out_specs=P("seq", "head"), check_vma=False
    )
```

profile of v0, /device:TPU:1, one launch (start us, length us, event | category | flops | bytes accessed | tf_op | source)
XLA Modules:
  0.0 558.2 jit_solution(9154548821410170501)
XLA Ops:
  6.5 1.0 copy.18
  7.5 0.9 copy.16
  8.5 0.7 compare_bitcast_fusion
  9.1 0.1 broadcast_select_fusion
  9.3 4.5 collective-permute-start
  13.8 1.9 collective-permute-start.14
  15.7 3.5 collective-permute-start.7
  19.2 0.7 fusion.25
  19.9 0.7 fusion.30
  30.8 1.9 fusion.20
  32.7 0.0 reduce-scatter.2.cloned.1.call-start
  32.8 0.7 compare_bitcast_fusion.1
  33.4 0.7 subtract_bitcast_fusion
  34.1 0.1 broadcast_in_dim.281
  34.2 0.2 and_reduce_fusion
  34.4 0.1 broadcast_bitcast_fusion
  34.5 0.3 pad_add_fusion
  34.8 1.4 fusion.29
  42.1 2.8 collective-permute-start.1
  45.4 319.1 %all-reduce.3.cloned.1.call-done = (bf16[1,128,2,128]{3,2,1,0:T(2,128)(2,1)}, bf16[1,128,2,128]{3,2,1,0:T(2,128)(2,1)}, bf16[1,128,2,128]{3,2,1,0:T(2,128)(2,1)}, bf16[1,128,2,128]{3,2,1,0:T(2,128)(2,1)}) async-done(((bf16[1,128,2,128]{3,2,1,0:T(2,128)(2,1)}, bf16[1,128,2,128]{3,2,1,0:T(2,128)(2,1)}, bf16[1,128,2,128]{3,2,1,0:T(2,128)(2,1)}, bf16[1,128,2,128]{3,2,1,0:T(2,128)(2,1)}), ...) | async-done | bytes 262160 | tf_op jit(solution)/shard_map/psum | solution.py:17
  364.5 1.4 pad_maximum_fusion.2
  366.0 2.8 collective-permute-start.8
  368.7 2.4 collective-permute-start.15
  371.2 4.5 collective-permute-start.2
  375.7 2.0 collective-permute-start.9
  377.7 0.8 collective-permute-done.15
  378.5 4.4 collective-permute-start.16
  382.9 4.2 collective-permute-start.3
  387.2 1.9 collective-permute-start.10
  389.2 2.7 collective-permute-start.17
  391.9 5.5 collective-permute-start.4
  397.4 2.6 collective-permute-start.11
  400.0 3.9 collective-permute-start.18
  404.0 3.9 collective-permute-start.5
  407.9 6.1 %collective-permute-start.12 = (bf16[1,256,2,128]{3,1,0,2:T(8,128)(2,1)S(1)}, bf16[1,256,2,128]{3,1,0,2:T(8,128)(2,1)S(1)}, u32[]{:S(2)}, u32[]{:S(2)}) collective-permute-start(bf16[1,256,2,128]{3,1,0,2:T(8,128)(2,1)S(1)} %broadcast_select_fusion.16), channel_id=1, source_target_pairs={{0,128},{4,132},{8,136},{12,140},{16,144},{20,148},{24,152},{28,15... | collective-permute-start | bytes 393224 | tf_op jit(solution)/shard_map/ppermute | solution.py:12
  414.1 4.2 collective-permute-start.19
  418.3 8.7 %collective-permute-start.6 = (bf16[1,256,2,128]{3,1,0,2:T(8,128)(2,1)S(1)}, bf16[1,256,2,128]{3,1,0,2:T(8,128)(2,1)S(1)}, u32[]{:S(2)}, u32[]{:S(2)}) collective-permute-start(bf16[1,256,2,128]{3,1,0,2:T(8,128)(2,1)S(1)} %broadcast_select_fusion.24), channel_id=1, source_target_pairs={{0,256},{4,260},{8,264},{12,268},{16,272},{20,276},{24,280},{28,28... | collective-permute-start | bytes 393224 | tf_op jit(solution)/shard_map/ppermute | solution.py:12
  427.0 5.3 collective-permute-start.13
  432.4 8.7 %collective-permute-start.20 = (bf16[1,256,2,128]{3,1,0,2:T(8,128)(2,1)S(1)}, bf16[1,256,2,128]{3,1,0,2:T(8,128)(2,1)S(1)}, u32[]{:S(2)}, u32[]{:S(2)}) collective-permute-start(bf16[1,256,2,128]{3,1,0,2:T(8,128)(2,1)S(1)} %broadcast_select_fusion.10), channel_id=1, source_target_pairs={{0,256},{4,260},{8,264},{12,268},{16,272},{20,276},{24,280},{28,28... | collective-permute-start | bytes 393224 | tf_op jit(solution)/shard_map/ppermute | solution.py:12
  441.1 10.1 %collective-permute-done.13 = bf16[1,256,2,128]{3,1,0,2:T(8,128)(2,1)S(1)} collective-permute-done((bf16[1,256,2,128]{3,1,0,2:T(8,128)(2,1)S(1)}, bf16[1,256,2,128]{3,1,0,2:T(8,128)(2,1)S(1)}, u32[]{:S(2)}, u32[]{:S(2)}) %collective-permute-start.13) | collective-permute-done | bytes 131104 | tf_op jit(solution)/shard_map/ppermute | solution.py:12
  451.2 10.7 %collective-permute-done.20 = bf16[1,256,2,128]{3,1,0,2:T(8,128)(2,1)S(1)} collective-permute-done((bf16[1,256,2,128]{3,1,0,2:T(8,128)(2,1)S(1)}, bf16[1,256,2,128]{3,1,0,2:T(8,128)(2,1)S(1)}, u32[]{:S(2)}, u32[]{:S(2)}) %collective-permute-start.20) | collective-permute-done | bytes 131104 | tf_op jit(solution)/shard_map/ppermute | solution.py:12
  461.9 0.1 pad_maximum_fusion
  462.0 6.9 %fusion.32 = (f32[8,256]{1,0:T(8,128)S(1)}, f32[8,256,1536]{1,2,0:T(8,128)}) fusion(pred[256,1536]{0,1:T(8,128)(4,1)S(1)} %pad_add_fusion, bf16[1536,2,128]{2,0,1:T(8,128)(2,1)S(1)} %pad_maximum_fusion, bf16[256,1024]{1,0:T(8,128)(2,1)S(1)} %copy-done), kind=kOutput, calls=%fused_computation.74 | convolution fusion | flops 817890816 | bytes 13901824 | tf_op jit(solution)/shard_map/sub | solution.py:81
  468.9 5.7 %fusion.8 = bf16[128,8,256]{2,0,1:T(8,128)(2,1)S(1)} fusion(f32[8,256,1536]{1,2,0:T(8,128)} %get-tuple-element.35, f32[8,256]{1,0:T(8,128)S(1)} %get-tuple-element.34, bf16[1536,2,128]{2,0,1:T(8,128)(2,1)S(1)} %pad_maximum_fusion), kind=kOutput, calls=%fused_computation.11 | convolution fusion | flops 811859968 | bytes 13508608 | tf_op jit(solution)/shard_map/grk,kd->rgd/dot_general | solution.py:84
  474.6 0.0 copy-done.1
  474.7 2.6 fusion.37
  477.3 72.3 %reduce-scatter.2.cloned.1.call-done = f32[256,512]{1,0:T(8,128)} async-done(((f32[256,2048]{1,0:T(8,128)}), f32[256,512]{1,0:T(8,128)}) %reduce-scatter.2.cloned.1.call-update) | async-done | bytes 524304 | tf_op jit(solution)/shard_map/reduce_scatter | solution.py:89
  549.6 1.8 convert_element_type.20
  (51 shorter events, 0.6 us)
Async XLA Ops:
  6.5 455.4 %copy-start = (bf16[256,1024]{1,0:T(8,128)(2,1)S(1)}, bf16[256,1024]{1,0:T(8,128)(2,1)}, u32[]{:S(2)}) copy-start(bf16[256,1024]{1,0:T(8,128)(2,1)} %param.7) | copy-start | bytes 1572868
  6.5 358.0 %all-reduce.3.cloned.1.call-start = ((), (), s32[]{:S(2)}) async-start(), calls=%async_computation.2 | async-start | bytes 524288 | tf_op jit(solution)/shard_map/psum | solution.py:17
  9.3 32.7 %collective-permute-start = (bf16[1,256,2,128]{3,1,0,2:T(8,128)(2,1)S(1)}, bf16[1,256,2,128]{3,1,0,2:T(8,128)(2,1)S(1)}, u32[]{:S(2)}, u32[]{:S(2)}) collective-permute-start(bf16[1,256,2,128]{3,1,0,2:T(8,128)(2,1)S(1)} %get-tuple-element.12), channel_id=1, source_target_pairs={{0,4},{4,8},{8,12},{12,16},{16,20},{20,24},{24,28},{28,32},{32,36}... | collective-permute-start | bytes 393224 | tf_op jit(solution)/shard_map/ppermute | solution.py:12
  13.8 28.2 %collective-permute-start.14 = (bf16[1,256,2,128]{3,1,0,2:T(8,128)(2,1)S(1)}, bf16[1,256,2,128]{3,1,0,2:T(8,128)(2,1)S(1)}, u32[]{:S(2)}, u32[]{:S(2)}) collective-permute-start(bf16[1,256,2,128]{3,1,0,2:T(8,128)(2,1)S(1)} %get-tuple-element.13), channel_id=1, source_target_pairs={{0,4},{4,8},{8,12},{12,16},{16,20},{20,24},{24,28},{28,32},{32,36}... | collective-permute-start | bytes 393224 | tf_op jit(solution)/shard_map/ppermute | solution.py:12
  15.7 26.3 %collective-permute-start.7 = (bf16[1,256,2,128]{3,1,0,2:T(8,128)(2,1)S(1)}, bf16[1,256,2,128]{3,1,0,2:T(8,128)(2,1)S(1)}, u32[]{:S(2)}, u32[]{:S(2)}) collective-permute-start(bf16[1,256,2,128]{3,1,0,2:T(8,128)(2,1)S(1)} %get-tuple-element.14), channel_id=1, source_target_pairs={{0,4},{4,8},{8,12},{12,16},{16,20},{20,24},{24,28},{28,32},{32,36}... | collective-permute-start | bytes 393224 | tf_op jit(solution)/shard_map/ppermute | solution.py:12
  32.7 516.9 %reduce-scatter.2.cloned.1.call-start = ((), (), s32[]{:S(2)}) async-start(), calls=%async_computation.1 | async-start | bytes 2621440 | tf_op jit(solution)/shard_map/reduce_scatter | solution.py:89
  42.1 329.1 %collective-permute-start.1 = (bf16[1,256,2,128]{3,1,0,2:T(8,128)(2,1)S(1)}, bf16[1,256,2,128]{3,1,0,2:T(8,128)(2,1)S(1)}, u32[]{:S(2)}, u32[]{:S(2)}) collective-permute-start(bf16[1,256,2,128]{3,1,0,2:T(8,128)(2,1)S(1)} %get-tuple-element.9), channel_id=1, source_target_pairs={{0,8},{4,12},{8,16},{12,20},{16,24},{20,28},{24,32},{28,36},{32,40... | collective-permute-start | bytes 393224 | tf_op jit(solution)/shard_map/ppermute | solution.py:12
  366.0 9.7 %collective-permute-start.8 = (bf16[1,256,2,128]{3,1,0,2:T(8,128)(2,1)S(1)}, bf16[1,256,2,128]{3,1,0,2:T(8,128)(2,1)S(1)}, u32[]{:S(2)}, u32[]{:S(2)}) collective-permute-start(bf16[1,256,2,128]{3,1,0,2:T(8,128)(2,1)S(1)} %get-tuple-element.10), channel_id=1, source_target_pairs={{0,8},{4,12},{8,16},{12,20},{16,24},{20,28},{24,32},{28,36},{32,40... | collective-permute-start | bytes 393224 | tf_op jit(solution)/shard_map/ppermute | solution.py:12
  368.7 9.7 %collective-permute-start.15 = (bf16[1,256,2,128]{3,1,0,2:T(8,128)(2,1)S(1)}, bf16[1,256,2,128]{3,1,0,2:T(8,128)(2,1)S(1)}, u32[]{:S(2)}, u32[]{:S(2)}) collective-permute-start(bf16[1,256,2,128]{3,1,0,2:T(8,128)(2,1)S(1)} %get-tuple-element.11), channel_id=1, source_target_pairs={{0,8},{4,12},{8,16},{12,20},{16,24},{20,28},{24,32},{28,36},{32,40... | collective-permute-start | bytes 393224 | tf_op jit(solution)/shard_map/ppermute | solution.py:12
  371.2 11.7 %collective-permute-start.2 = (bf16[1,256,2,128]{3,1,0,2:T(8,128)(2,1)S(1)}, bf16[1,256,2,128]{3,1,0,2:T(8,128)(2,1)S(1)}, u32[]{:S(2)}, u32[]{:S(2)}) collective-permute-start(bf16[1,256,2,128]{3,1,0,2:T(8,128)(2,1)S(1)} %broadcast_select_fusion.20), channel_id=1, source_target_pairs={{0,16},{4,20},{8,24},{12,28},{16,32},{20,36},{24,40},{28,44},{32,4... | collective-permute-start | bytes 393224 | tf_op jit(solution)/shard_map/ppermute | solution.py:12
  375.7 11.5 %collective-permute-start.9 = (bf16[1,256,2,128]{3,1,0,2:T(8,128)(2,1)S(1)}, bf16[1,256,2,128]{3,1,0,2:T(8,128)(2,1)S(1)}, u32[]{:S(2)}, u32[]{:S(2)}) collective-permute-start(bf16[1,256,2,128]{3,1,0,2:T(8,128)(2,1)S(1)} %broadcast_select_fusion.13), channel_id=1, source_target_pairs={{0,16},{4,20},{8,24},{12,28},{16,32},{20,36},{24,40},{28,44},{32,4... | collective-permute-start | bytes 393224 | tf_op jit(solution)/shard_map/ppermute | solution.py:12
  378.5 10.6 %collective-permute-start.16 = (bf16[1,256,2,128]{3,1,0,2:T(8,128)(2,1)S(1)}, bf16[1,256,2,128]{3,1,0,2:T(8,128)(2,1)S(1)}, u32[]{:S(2)}, u32[]{:S(2)}) collective-permute-start(bf16[1,256,2,128]{3,1,0,2:T(8,128)(2,1)S(1)} %broadcast_select_fusion.6), channel_id=1, source_target_pairs={{0,16},{4,20},{8,24},{12,28},{16,32},{20,36},{24,40},{28,44},{32,4... | collective-permute-start | bytes 393224 | tf_op jit(solution)/shard_map/ppermute | solution.py:12
  382.9 8.9 %collective-permute-start.3 = (bf16[1,256,2,128]{3,1,0,2:T(8,128)(2,1)S(1)}, bf16[1,256,2,128]{3,1,0,2:T(8,128)(2,1)S(1)}, u32[]{:S(2)}, u32[]{:S(2)}) collective-permute-start(bf16[1,256,2,128]{3,1,0,2:T(8,128)(2,1)S(1)} %broadcast_select_fusion.21), channel_id=1, source_target_pairs={{0,32},{4,36},{8,40},{12,44},{16,48},{20,52},{24,56},{28,60},{32,6... | collective-permute-start | bytes 393224 | tf_op jit(solution)/shard_map/ppermute | solution.py:12
  387.2 10.2 %collective-permute-start.10 = (bf16[1,256,2,128]{3,1,0,2:T(8,128)(2,1)S(1)}, bf16[1,256,2,128]{3,1,0,2:T(8,128)(2,1)S(1)}, u32[]{:S(2)}, u32[]{:S(2)}) collective-permute-start(bf16[1,256,2,128]{3,1,0,2:T(8,128)(2,1)S(1)} %broadcast_select_fusion.14), channel_id=1, source_target_pairs={{0,32},{4,36},{8,40},{12,44},{16,48},{20,52},{24,56},{28,60},{32,6... | collective-permute-start | bytes 393224 | tf_op jit(solution)/shard_map/ppermute | solution.py:12
  389.2 10.8 %collective-permute-start.17 = (bf16[1,256,2,128]{3,1,0,2:T(8,128)(2,1)S(1)}, bf16[1,256,2,128]{3,1,0,2:T(8,128)(2,1)S(1)}, u32[]{:S(2)}, u32[]{:S(2)}) collective-permute-start(bf16[1,256,2,128]{3,1,0,2:T(8,128)(2,1)S(1)} %broadcast_select_fusion.7), channel_id=1, source_target_pairs={{0,32},{4,36},{8,40},{12,44},{16,48},{20,52},{24,56},{28,60},{32,6... | collective-permute-start | bytes 393224 | tf_op jit(solution)/shard_map/ppermute | solution.py:12
  391.9 12.1 %collective-permute-start.4 = (bf16[1,256,2,128]{3,1,0,2:T(8,128)(2,1)S(1)}, bf16[1,256,2,128]{3,1,0,2:T(8,128)(2,1)S(1)}, u32[]{:S(2)}, u32[]{:S(2)}) collective-permute-start(bf16[1,256,2,128]{3,1,0,2:T(8,128)(2,1)S(1)} %broadcast_select_fusion.22), channel_id=1, source_target_pairs={{0,64},{4,68},{8,72},{12,76},{16,80},{20,84},{24,88},{28,92},{32,9... | collective-permute-start | bytes 393224 | tf_op jit(solution)/shard_map/ppermute | solution.py:12
  397.4 10.5 %collective-permute-start.11 = (bf16[1,256,2,128]{3,1,0,2:T(8,128)(2,1)S(1)}, bf16[1,256,2,128]{3,1,0,2:T(8,128)(2,1)S(1)}, u32[]{:S(2)}, u32[]{:S(2)}) collective-permute-start(bf16[1,256,2,128]{3,1,0,2:T(8,128)(2,1)S(1)} %broadcast_select_fusion.15), channel_id=1, source_target_pairs={{0,64},{4,68},{8,72},{12,76},{16,80},{20,84},{24,88},{28,92},{32,9... | collective-permute-start | bytes 393224 | tf_op jit(solution)/shard_map/ppermute | solution.py:12
  400.0 14.0 %collective-permute-start.18 = (bf16[1,256,2,128]{3,1,0,2:T(8,128)(2,1)S(1)}, bf16[1,256,2,128]{3,1,0,2:T(8,128)(2,1)S(1)}, u32[]{:S(2)}, u32[]{:S(2)}) collective-permute-start(bf16[1,256,2,128]{3,1,0,2:T(8,128)(2,1)S(1)} %broadcast_select_fusion.8), channel_id=1, source_target_pairs={{0,64},{4,68},{8,72},{12,76},{16,80},{20,84},{24,88},{28,92},{32,9... | collective-permute-start | bytes 393224 | tf_op jit(solution)/shard_map/ppermute | solution.py:12
  404.0 14.2 %collective-permute-start.5 = (bf16[1,256,2,128]{3,1,0,2:T(8,128)(2,1)S(1)}, bf16[1,256,2,128]{3,1,0,2:T(8,128)(2,1)S(1)}, u32[]{:S(2)}, u32[]{:S(2)}) collective-permute-start(bf16[1,256,2,128]{3,1,0,2:T(8,128)(2,1)S(1)} %broadcast_select_fusion.23), channel_id=1, source_target_pairs={{0,128},{4,132},{8,136},{12,140},{16,144},{20,148},{24,152},{28,15... | collective-permute-start | bytes 393224 | tf_op jit(solution)/shard_map/ppermute | solution.py:12
  407.9 19.1 %collective-permute-start.12 = (bf16[1,256,2,128]{3,1,0,2:T(8,128)(2,1)S(1)}, bf16[1,256,2,128]{3,1,0,2:T(8,128)(2,1)S(1)}, u32[]{:S(2)}, u32[]{:S(2)}) collective-permute-start(bf16[1,256,2,128]{3,1,0,2:T(8,128)(2,1)S(1)} %broadcast_select_fusion.16), channel_id=1, source_target_pairs={{0,128},{4,132},{8,136},{12,140},{16,144},{20,148},{24,152},{28,15... | collective-permute-start | bytes 393224 | tf_op jit(solution)/shard_map/ppermute | solution.py:12
  414.1 18.3 %collective-permute-start.19 = (bf16[1,256,2,128]{3,1,0,2:T(8,128)(2,1)S(1)}, bf16[1,256,2,128]{3,1,0,2:T(8,128)(2,1)S(1)}, u32[]{:S(2)}, u32[]{:S(2)}) collective-permute-start(bf16[1,256,2,128]{3,1,0,2:T(8,128)(2,1)S(1)} %broadcast_select_fusion.9), channel_id=1, source_target_pairs={{0,128},{4,132},{8,136},{12,140},{16,144},{20,148},{24,152},{28,15... | collective-permute-start | bytes 393224 | tf_op jit(solution)/shard_map/ppermute | solution.py:12
  418.3 22.8 %collective-permute-start.6 = (bf16[1,256,2,128]{3,1,0,2:T(8,128)(2,1)S(1)}, bf16[1,256,2,128]{3,1,0,2:T(8,128)(2,1)S(1)}, u32[]{:S(2)}, u32[]{:S(2)}) collective-permute-start(bf16[1,256,2,128]{3,1,0,2:T(8,128)(2,1)S(1)} %broadcast_select_fusion.24), channel_id=1, source_target_pairs={{0,256},{4,260},{8,264},{12,268},{16,272},{20,276},{24,280},{28,28... | collective-permute-start | bytes 393224 | tf_op jit(solution)/shard_map/ppermute | solution.py:12
  427.0 24.1 %collective-permute-start.13 = (bf16[1,256,2,128]{3,1,0,2:T(8,128)(2,1)S(1)}, bf16[1,256,2,128]{3,1,0,2:T(8,128)(2,1)S(1)}, u32[]{:S(2)}, u32[]{:S(2)}) collective-permute-start(bf16[1,256,2,128]{3,1,0,2:T(8,128)(2,1)S(1)} %broadcast_select_fusion.17), channel_id=1, source_target_pairs={{0,256},{4,260},{8,264},{12,268},{16,272},{20,276},{24,280},{28,28... | collective-permute-start | bytes 393224 | tf_op jit(solution)/shard_map/ppermute | solution.py:12
  432.4 29.5 %collective-permute-start.20 = (bf16[1,256,2,128]{3,1,0,2:T(8,128)(2,1)S(1)}, bf16[1,256,2,128]{3,1,0,2:T(8,128)(2,1)S(1)}, u32[]{:S(2)}, u32[]{:S(2)}) collective-permute-start(bf16[1,256,2,128]{3,1,0,2:T(8,128)(2,1)S(1)} %broadcast_select_fusion.10), channel_id=1, source_target_pairs={{0,256},{4,260},{8,264},{12,268},{16,272},{20,276},{24,280},{28,28... | collective-permute-start | bytes 393224 | tf_op jit(solution)/shard_map/ppermute | solution.py:12
  468.9 5.8 %copy-start.1 = (bf16[1024,2048]{1,0:T(8,128)(2,1)S(1)}, bf16[1024,2048]{1,0:T(8,128)(2,1)}, u32[]{:S(2)}) copy-start(bf16[1024,2048]{1,0:T(8,128)(2,1)} %param.13) | copy-start | bytes 12582916
Sparse Core Ops, SparseCore 0:
  32.8 331.6 all-reduce.2
  477.4 72.1 reduce-scatter.1
where the time goes:
time: 559 us; the launch traced here: 558 us
  waiting for transfers between devices  413 us (74%)
  starting transfers between devices  86.4 us (15%)
  between operations  30.4 us (5%)
  matrix products  15.3 us (3%)
  other arithmetic  8.8 us (2%)
    psum x1, waiting for transfers between devices, broadcast(): return lax.psum(kept, axis)  319 us
    ppermute x21, starting transfers between devices, passed_along(): return lax.ppermute(value, axis, pairs)  86.4 us
    reduce_scatter x1, waiting for transfers between devices, body(): lax.psum_scatter(group_terms, 'head', scatter_dimension=1, tiled=True)  72.3 us
    ppermute x21, waiting for transfers between devices, passed_along(): return lax.ppermute(value, axis, pairs)  21.6 us
  transfers between devices with their start and end apart: 23, of which 5 were waited for; matrix products, arithmetic and copies ran while one was open for 2% of the time, Pallas kernels for 0%

commit v1 on v0

v1 whole, which is shorter than its diff:
```python
import functools

import jax
import jax.numpy as jnp
from jax import lax
from jax.experimental import pallas as pl
from jax.experimental.pallas import tpu as pltpu
from jax.sharding import PartitionSpec as P

MESH = pl.DeviceIdType.MESH
NC = 4
NZ, NX = 16, 4
CR = 32
KC = 3 * 2 * CR + 4 * CR
NEG = -1e30


def place():
    s = lax.axis_index("seq")
    return s // 8, (s // 2) % NX, s % 2, lax.axis_index("head")


def at(z, x, c, y):
    return (lax.rem(z + NZ, NZ) * 8 + lax.rem(x + NX, NX) * 2 + lax.rem(c + 2, 2), y)


def fetch_kernel(shift, pages, src, out, *scratch):
    zb, xb = scratch[:NC], scratch[NC : 2 * NC]
    sel, cs, cr = (scratch[2 * NC + NC * i : 2 * NC + NC * (i + 1)] for i in range(3))
    zsend, zrecv, xsend, xrecv = scratch[5 * NC :]
    z, x, c, y = place()
    j = x * 2 + c
    up, down = at(z + 1, x, c, y), at(z - 1, x, c, y)
    right, left = at(z, x + 1, c, y), at(z, x - 1, c, y)
    twin = at(z, x, 1 - c, y)

    bar = pltpu.get_barrier_semaphore()
    for peer in (up, down, right, left, twin):
        pl.semaphore_signal(bar, inc=1, device_id=peer, device_id_type=MESH)
    for ch in range(NC):
        zb[ch][z] = src[ch]
    pl.semaphore_wait(bar, 5)

    started = []

    def zcopy(ch, way, hop):
        block = lax.rem(z + NZ - hop, NZ) if way == 0 else lax.rem(z + hop, NZ)
        view = zb[ch].at[block] if hop < 7 else zb[ch].at[block, way]
        return pltpu.make_async_remote_copy(
            src_ref=view, dst_ref=view,
            send_sem=zsend.at[ch, way, hop], recv_sem=zrecv.at[ch, way, hop],
            device_id=up if way == 0 else down, device_id_type=MESH,
        )

    def zarrive(ch, way, hop):
        block = lax.rem(z + NZ - hop - 1, NZ) if way == 0 else lax.rem(z + hop + 1, NZ)
        view = zb[ch].at[block] if hop < 7 else zb[ch].at[block, way]
        pltpu.make_async_remote_copy(
            src_ref=view, dst_ref=view,
            send_sem=zsend.at[ch, way, hop], recv_sem=zrecv.at[ch, way, hop],
            device_id=up if way == 0 else down, device_id_type=MESH,
        ).wait_recv()

    def zstep(ch, hop):
        for way in range(2):
            if hop > 0:
                zarrive(ch, way, hop - 1)
            cp = zcopy(ch, way, hop)
            cp.start()
            started.append(cp)

    def send(ch, slot, view, dst, to):
        cp = pltpu.make_async_remote_copy(
            src_ref=view, dst_ref=dst, send_sem=xsend.at[ch, slot], recv_sem=xrecv.at[ch, slot],
            device_id=to, device_id_type=MESH,
        )
        cp.start()
        started.append(cp)

    def arrive(ch, slot, dst, to):
        pltpu.make_async_remote_copy(
            src_ref=dst, dst_ref=dst, send_sem=xsend.at[ch, slot], recv_sem=xrecv.at[ch, slot],
            device_id=to, device_id_type=MESH,
        ).wait_recv()

    def xstep(ch, step):
        xl, xr, xo = lax.rem(x + 3, NX), lax.rem(x + 1, NX), lax.rem(x + 2, NX)
        if step == 0:
            for way in range(2):
                zarrive(ch, way, 7)
            for k in range(3):
                d = shift[0, k]
                r, q = lax.rem(d, 8), d // 8
                m = q + jnp.where(j + r >= 8, 1, 0)
                from_slab = z - m >= 0
                zs = lax.rem(z - m + 2 * NZ, NZ)
                got = zb[ch][zs, jnp.where(from_slab, 0, 1)]
                sel[ch][k * 2 * CR : (k + 1) * 2 * CR] = got[0].reshape(2 * CR, 128)
                sel[ch][KC + k * 2 * CR : KC + (k + 1) * 2 * CR] = got[1].reshape(2 * CR, 128)
            for i in range(4):
                p = pages[0, i]
                got = zb[ch][p // 16, 1, :, lax.rem(p, 2)]
                lo = 6 * CR + i * CR
                sel[ch][lo : lo + CR] = got[0]
                sel[ch][KC + lo : KC + lo + CR] = got[1]
            xb[ch][x] = sel[ch][...]
            send(ch, 0, sel[ch], xb[ch].at[x], right)
            send(ch, 1, sel[ch], xb[ch].at[x], left)
        if step == 1:
            arrive(ch, 0, xb[ch].at[xl], right)
            lo = xb[ch].at[xl, pl.ds(0, KC)]
            send(ch, 2, lo, lo, right)
            arrive(ch, 1, xb[ch].at[xr], left)
            hi = xb[ch].at[xr, pl.ds(KC, KC)]
            send(ch, 3, hi, hi, left)
        if step == 2:
            arrive(ch, 2, xb[ch].at[xo, pl.ds(0, KC)], right)
            arrive(ch, 3, xb[ch].at[xo, pl.ds(KC, KC)], left)
            for who, put in ((j, out.at[ch]), (lax.rem(j + 1, 2) + (j // 2) * 2, cs[ch])):
                for k in range(3):
                    r = lax.rem(shift[0, k], 8)
                    xs = lax.rem(who - r + 8, 8) // 2
                    for half in range(2):
                        lo = half * KC + k * 2 * CR
                        put[lo : lo + 2 * CR] = xb[ch][xs, lo : lo + 2 * CR]
                for i in range(4):
                    xs = lax.rem(pages[0, i] // 2, 8) // 2
                    for half in range(2):
                        lo = half * KC + 6 * CR + i * CR
                        put[lo : lo + CR] = xb[ch][xs, lo : lo + CR]
            send(ch, 4, cs[ch], cr[ch], twin)
        if step == 3:
            arrive(ch, 4, cr[ch], twin)
            for k in range(3):
                r = lax.rem(shift[0, k], 8)
                mine = lax.rem(lax.rem(j - r + 8, 8), 2) == c
                for half in range(2):
                    lo = half * KC + k * 2 * CR
                    out[ch, lo : lo + 2 * CR] = jnp.where(
                        mine, out[ch, lo : lo + 2 * CR], cr[ch][lo : lo + 2 * CR]
                    )
            for i in range(4):
                mine = lax.rem(pages[0, i] // 2, 2) == c
                for half in range(2):
                    lo = half * KC + 6 * CR + i * CR
                    out[ch, lo : lo + CR] = jnp.where(
                        mine, out[ch, lo : lo + CR], cr[ch][lo : lo + CR]
                    )

    for hop in range(8):
        for ch in (0, 1):
            zstep(ch, hop)
    for hop in range(8):
        for ch in (2, 3):
            zstep(ch, hop)
        if hop in (0, 2, 4, 6):
            xstep(0, hop // 2)
        if hop in (1, 3, 5, 7):
            xstep(1, hop // 2)
    for step in range(4):
        for ch in (2, 3):
            xstep(ch, step)
    for cp in started:
        cp.wait_send()


def fetch(shift, pages, src):
    smem = pl.BlockSpec(memory_space=pltpu.SMEM)
    vmem = pl.BlockSpec(memory_space=pltpu.VMEM)
    bf = jnp.bfloat16
    return pl.pallas_call(
        fetch_kernel,
        name="fetch",
        out_shape=jax.ShapeDtypeStruct((NC, 2 * KC, 128), bf),
        in_specs=[smem, smem, vmem],
        out_specs=vmem,
        scratch_shapes=[pltpu.VMEM((NZ, 2, 2, 2, CR, 128), bf)] * NC
        + [pltpu.VMEM((NX, 2 * KC, 128), bf)] * NC
        + [pltpu.VMEM((2 * KC, 128), bf)] * (3 * NC)
        + [pltpu.SemaphoreType.DMA((NC, 2, 8))] * 2
        + [pltpu.SemaphoreType.DMA((NC, 5))] * 2,
        compiler_params=pltpu.CompilerParams(
            collective_id=0, has_side_effects=True, vmem_limit_bytes=48 * 2**20
        ),
    )(shift, pages, src)


def attend_kernel(shift, pages, live, q, src, got, att):
    s = lax.axis_index("seq")
    own = NC * 2 * CR
    scale = 128**-0.5 * 1.4426950408889634
    rows = lax.broadcasted_iota(jnp.int32, (own, own), 0)
    at_ = lax.broadcasted_iota(jnp.int32, (own, own), 1)
    cols = (at_ // CR) % 2 * 128 + at_ // (2 * CR) * CR + at_ % CR
    causal = rows >= cols
    lane = lax.broadcasted_iota(jnp.int32, (1, KC), 1)
    bias = jnp.zeros((1, KC), jnp.float32)
    for k in range(3):
        here = (lane >= k * 2 * CR) & (lane < (k + 1) * 2 * CR)
        bias = jnp.where(here & (live[0, k] != 1), NEG, bias)
    for i in range(4):
        shut = False
        for k in range(3):
            d = shift[0, k]
            shut = shut | ((live[0, k] == 1) & (d > s) & (s + 128 - d == pages[0, i] // 2))
        here = (lane >= 6 * CR + i * CR) & (lane < 6 * CR + (i + 1) * CR)
        bias = jnp.where(here & shut, NEG, bias)
    bias = jnp.concatenate([bias] * NC, 1)
    keys0 = jnp.concatenate([src[ch, 0, 0].reshape(2 * CR, 128) for ch in range(NC)], 0)
    vals0 = jnp.concatenate([src[ch, 0, 1].reshape(2 * CR, 128) for ch in range(NC)], 0)
    keys1 = jnp.concatenate([got[ch, :KC] for ch in range(NC)], 0)
    vals1 = jnp.concatenate([got[ch, KC:] for ch in range(NC)], 0)
    contract = (((1,), (1,)), ((), ()))
    for h in range(8):
        qh = q[:, h * 128 : (h + 1) * 128]
        s0 = lax.dot_general(qh, keys0, contract, preferred_element_type=jnp.float32)
        s1 = lax.dot_general(qh, keys1, contract, preferred_element_type=jnp.float32)
        s0 = jnp.where(causal, s0, NEG)
        s1 = s1 + bias
        top = jnp.maximum(jnp.max(s0, 1, keepdims=True), jnp.max(s1, 1, keepdims=True))
        e0 = jnp.exp2((s0 - top) * scale)
        e1 = jnp.exp2((s1 - top) * scale)
        total = jnp.sum(e0, 1, keepdims=True) + jnp.sum(e1, 1, keepdims=True)
        o = jnp.dot(e0.astype(jnp.bfloat16), vals0, preferred_element_type=jnp.float32)
        o += jnp.dot(e1.astype(jnp.bfloat16), vals1, preferred_element_type=jnp.float32)
        att[:, h * 128 : (h + 1) * 128] = (o / total).astype(jnp.bfloat16)


def attend(shift, pages, live, q, src, got):
    smem = pl.BlockSpec(memory_space=pltpu.SMEM)
    vmem = pl.BlockSpec(memory_space=pltpu.VMEM)
    return pl.pallas_call(
        attend_kernel,
        name="attend",
        out_shape=jax.ShapeDtypeStruct(q.shape, jnp.bfloat16),
        in_specs=[smem, smem, smem, vmem, vmem, vmem],
        out_specs=vmem,
        compiler_params=pltpu.CompilerParams(vmem_limit_bytes=48 * 2**20),
    )(shift, pages, live, q, src, got)


def project_kernel(att, w, out, parts, inbox, ssem, rsem):
    s, y = lax.axis_index("seq"), lax.axis_index("head")
    bar = pltpu.get_barrier_semaphore()
    for step in (1, 2, 3):
        pl.semaphore_signal(
            bar, inc=1, device_id=(s, lax.rem(y + step, 4)), device_id_type=MESH
        )
    pl.semaphore_wait(bar, 3)
    a = att[...]
    sends = []
    for step in (2, 1, 3):
        to = lax.rem(y + step, 4)
        cols = pl.ds(pl.multiple_of(to * 512, 512), 512)
        parts[step - 1] = jnp.dot(
            a, w[:, cols], preferred_element_type=jnp.float32
        ).astype(jnp.bfloat16)
        cp = pltpu.make_async_remote_copy(
            src_ref=parts.at[step - 1], dst_ref=inbox.at[step - 1],
            send_sem=ssem.at[step - 1], recv_sem=rsem.at[step - 1],
            device_id=(s, to), device_id_type=MESH,
        )
        cp.start()
        sends.append(cp)
    total = jnp.dot(
        a, w[:, pl.ds(pl.multiple_of(y * 512, 512), 512)], preferred_element_type=jnp.float32
    )
    for cp, step in zip(sends, (2, 1, 3)):
        cp.wait()
    out[...] = (
        total + inbox[0].astype(jnp.float32) + inbox[1].astype(jnp.float32)
        + inbox[2].astype(jnp.float32)
    ).astype(jnp.bfloat16)


def project(att, w):
    vmem = pl.BlockSpec(memory_space=pltpu.VMEM)
    return pl.pallas_call(
        project_kernel,
        name="project",
        out_shape=jax.ShapeDtypeStruct((att.shape[0], 512), jnp.bfloat16),
        in_specs=[vmem, vmem],
        out_specs=vmem,
        scratch_shapes=[
            pltpu.VMEM((3, att.shape[0], 512), jnp.bfloat16),
            pltpu.VMEM((3, att.shape[0], 512), jnp.bfloat16),
            pltpu.SemaphoreType.DMA((3,)),
            pltpu.SemaphoreType.DMA((3,)),
        ],
        compiler_params=pltpu.CompilerParams(
            collective_id=1, has_side_effects=True, vmem_limit_bytes=48 * 2**20
        ),
    )(att, w)


def chunked(kv):
    return kv.reshape(2, NC, CR, 2, 128).transpose(1, 3, 0, 2, 4)


def body(queries, keys_values, cache_kv, vertical_pages, slash_shift, slash_live, out_proj):
    src = jnp.stack([chunked(keys_values), chunked(cache_kv)], 1)
    got = fetch(slash_shift, vertical_pages, src)
    att = attend(slash_shift, vertical_pages, slash_live[0], queries, src, got)
    return project(att, out_proj)


def solution(mesh):
    placed = (
        P("seq", "head"),
        P("seq", None, "head"),
        P("seq", None, "head"),
        P("head", None),
        P("head", None),
        P("seq", "head", None),
        P("head", None),
    )
    return jax.shard_map(
        body, mesh=mesh, in_specs=placed, out_specs=P("seq", "head"), check_vma=False
    )
```

time: 559 us -> 116 us (0.21)
  waiting for transfers between devices: 413 us -> 0 us
  Pallas kernels: 0 us -> 109 us
  starting transfers between devices: 86.4 us -> 0 us
  between operations: 30.4 us -> 0.07 us
  matrix products: 15.3 us -> 0 us
  other arithmetic: 8.8 us -> 0.03 us
    psum x1 -> x0, waiting for transfers between devices: 319 us -> none  [broadcast(): return lax.psum(kept, axis)]
    pallas_call x0 -> x3, Pallas kernels: none -> 109 us  [the longest x1 84.7 us: fetch(): pl.pallas_call(fetch_kernel, name='fetch', out_shape=jax.ShapeDtypeStruct...]
    ppermute x21 -> x0, starting transfers between devices: 86.4 us -> none  [passed_along(): return lax.ppermute(value, axis, pairs)]
    reduce_scatter x1 -> x0, waiting for transfers between devices: 72.3 us -> none  [body(): lax.psum_scatter(group_terms, 'head', scatter_dimension=1, tiled=True)]
    ppermute x21 -> x0, waiting for transfers between devices: 21.6 us -> none  [passed_along(): return lax.ppermute(value, axis, pairs)]
    dot_general x2 -> x0, matrix products: 8.35 us -> none  [the longest x1 5.73 us: body(): jnp.einsum('grk,kd->rgd', weights_bf, all_keys[:, 1, :], preferred_elemen...]
    sub x1 -> x0, matrix products: 6.91 us -> none  [body(): weights = jnp.exp(scores - row_max)]
  transfers between devices with their start and end apart: 23 -> 0, of which waited for: 5 -> 0; matrix products, arithmetic and copies ran while one was open for 2% -> 0% of each run, Pallas kernels for 0% -> 0%
where the time goes in v1:
time: 116 us
  Pallas kernels  109 us (94%)
  local copies, waits for them, and re-layouts  6.9 us (6%)
    pallas_call x1, Pallas kernels, fetch(): pl.pallas_call(fetch_kernel, name='fetch', out_shape=jax.ShapeDtypeStruct...  84.7 us
    pallas_call x1, Pallas kernels, project(): pl.pallas_call(project_kernel, name='project', out_shape=jax.ShapeDtypeSt...  18 us
    pallas_call x1, Pallas kernels, attend(): pl.pallas_call(attend_kernel, name='attend', out_shape=jax.ShapeDtypeStru...  6.16 us
    unnamed x11, local copies, waits for them, and re-layouts  5.89 us

profile of v1, /device:TPU:1, one launch (start us, length us, event | category | flops | bytes accessed | tf_op | source)
XLA Modules:
  0.0 115.8 jit_solution(4263894175289076393)
XLA Ops:
  0.0 1.0 copy_bitcast_fusion
  1.1 0.0 copy-start.2
  1.1 0.6 copy-done.2
  1.7 0.0 copy-start.3
  1.7 0.7 copy-done.3
  2.4 84.7 %fetch.1.got = bf16[4,640,128]{2,1,0:T(8,128)(2,1)S(1)} custom-call(s32[1,3]{1,0:T(1,128)S(1)} %copy-done.2, s32[1,4]{1,0:T(1,128)S(1)} %copy-done.3, bf16[4,2,2,2,32,128]{5,4,3,2,1,0:T(8,128)(2,1)S(1)} %pad_maximum_fusion.src), custom_call_target="tpu_custom_call" | custom-call | tf_op jit(solution)/shard_map/fetch/pallas_call | solution.py:171
  87.0 0.0 copy-start.1
  87.1 1.0 copy-done.1
  88.1 0.0 copy-start.4
  88.1 0.7 copy-done.4
  88.7 6.2 %attend.1.att = bf16[256,1024]{1,0:T(8,128)(2,1)S(1)} custom-call(s32[1,3]{1,0:T(1,128)S(1)} %copy-done.2, s32[1,4]{1,0:T(1,128)S(1)} %copy-done.3, s32[1,3]{1,0:T(1,128)S(1)} %bitcast.11, bf16[256,1024]{1,0:T(8,128)(2,1)S(1)} %copy-done.1, bf16[4,2,2,2,32,128]{5,4,3,2,1,0:T(8,128)(2,1)S(1)} %pad_maximum_fusion.src, bf16[4,640,128]{2,1,0:T(8,128)(2,1)S(1)} %fetch.1.got), custom_call_target="tpu_custom_call" | custom-call | tf_op jit(solution)/shard_map/attend/pallas_call | solution.py:232
  94.9 0.0 copy-start
  94.9 2.2 %copy-done = bf16[1024,2048]{1,0:T(8,128)(2,1)S(1)} copy-done((bf16[1024,2048]{1,0:T(8,128)(2,1)S(1)}, bf16[1024,2048]{1,0:T(8,128)(2,1)}, u32[]{:S(2)}) %copy-start) | copy-done | bytes 4194328
  97.1 18.0 %project.1 = bf16[256,512]{1,0:T(8,128)(2,1)S(1)} custom-call(bf16[256,1024]{1,0:T(8,128)(2,1)S(1)} %attend.1.att, bf16[1024,2048]{1,0:T(8,128)(2,1)S(1)} %copy-done), custom_call_target="tpu_custom_call" | custom-call | tf_op jit(solution)/shard_map/project/pallas_call | solution.py:278
  115.1 0.7 copy.19
  (1 shorter events, 0.0 us)
Async XLA Ops:
  1.1 0.7 copy-start.2
  1.7 0.7 copy-start.3
  87.0 1.0 copy-start.1
  88.1 0.7 copy-start.4
  94.9 2.2 %copy-start = (bf16[1024,2048]{1,0:T(8,128)(2,1)S(1)}, bf16[1024,2048]{1,0:T(8,128)(2,1)}, u32[]{:S(2)}) copy-start(bf16[1024,2048]{1,0:T(8,128)(2,1)} %w.1) | copy-start | bytes 12582916

commit v2 on v0

v2 whole, which is shorter than its diff:
```python
import functools

import jax
import jax.numpy as jnp
from jax import lax
from jax.experimental import pallas as pl
from jax.experimental.pallas import tpu as pltpu
from jax.sharding import PartitionSpec as P

MESH = pl.DeviceIdType.MESH
NC = 4
NZ, NX = 16, 4
NT = 4
CR = 32
KC = 3 * 2 * CR + 4 * CR
NEG = -1e30


def place():
    s = lax.axis_index("seq")
    return s // 8, (s // 2) % NX, s % 2, lax.axis_index("head")


def at(z, x, c, y):
    return (lax.rem(z + NZ, NZ) * 8 + lax.rem(x + NX, NX) * 2 + lax.rem(c + 2, 2), y)


SK = 3 * 2 * CR
PK = 4 * CR


def kernel(shift, pages, live, slab, cache, q_hbm, w_hbm, out, *scratch):
    zb = scratch[:NC]
    sel, tw, my, msg_l, fwd_r, fwd_l, a_l, a_r, b_l, b_r = (
        scratch[NC * (i + 1) : NC * (i + 2)] for i in range(10)
    )
    (psel, ptw, pg, pa_l, pa_r, pb_l, pb_r, pcol, pcol2,
     q, w, kall, vall, att, parts, inbox,
     zsend, zrecv, xsend, xrecv, psend, precv, ysend, yrecv, lsem) = scratch[11 * NC :]
    s = lax.axis_index("seq")
    z, x, c, y = place()
    j = x * 2 + c
    up, down = at(z + 1, x, c, y), at(z - 1, x, c, y)
    right, left = at(z, x + 1, c, y), at(z, x - 1, c, y)
    twin = at(z, x, 1 - c, y)

    bar = pltpu.get_barrier_semaphore()
    others = [(s, lax.rem(y + step, 4)) for step in (1, 2, 3)]
    up2, down2 = at(z + 2, x, c, y), at(z - 2, x, c, y)
    for peer in [up, down, down2, right, left, twin] + others:
        pl.semaphore_signal(bar, inc=1, device_id=peer, device_id_type=MESH)
    local = [
        pltpu.make_async_copy(q_hbm, q, lsem.at[0]),
        pltpu.make_async_copy(w_hbm, w, lsem.at[1]),
    ]
    for ch in range(NC):
        zb[ch][z, 0] = slab[ch].reshape(4 * CR, 128)
        zb[ch][z, 1] = cache[ch].reshape(4 * CR, 128)
    pl.semaphore_wait(bar, 9)

    started = []

    def zcopy(ch, way, hop, block):
        view = zb[ch].at[block] if hop < 7 else zb[ch].at[block, way]
        return pltpu.make_async_remote_copy(
            src_ref=view, dst_ref=view,
            send_sem=zsend.at[ch, way, hop], recv_sem=zrecv.at[ch, way, hop],
            device_id=up if way == 0 else down, device_id_type=MESH,
        )

    def zarrive(ch, way, hop):
        block = lax.rem(z + NZ - hop - 1, NZ) if way == 0 else lax.rem(z + hop + 1, NZ)
        zcopy(ch, way, hop, block).wait_recv()

    def zstep(ch, hop):
        for way in range(2):
            if hop > 0:
                zarrive(ch, way, hop - 1)
            block = lax.rem(z + NZ - hop, NZ) if way == 0 else lax.rem(z + hop, NZ)
            cp = zcopy(ch, way, hop, block)
            cp.start()
            started.append(cp)

    def xcopy(ch, slot, view, dst, to):
        return pltpu.make_async_remote_copy(
            src_ref=view, dst_ref=dst, send_sem=xsend.at[ch, slot], recv_sem=xrecv.at[ch, slot],
            device_id=to, device_id_type=MESH,
        )

    def send(ch, slot, view, dst, to):
        cp = xcopy(ch, slot, view, dst, to)
        cp.start()
        started.append(cp)

    def arrive(ch, slot, dst, to):
        xcopy(ch, slot, dst, dst, to).wait_recv()

    def turn(k):
        r = lax.rem(shift[0, k], 8)
        swap = lax.rem(r, 2) == 1
        rho = lax.rem(r // 2 + jnp.where(swap & (c == 0), 1, 0), NX)
        return rho, swap

    def xstep(ch, step):
        if step == 0:
            for way in range(2):
                zarrive(ch, way, 7)
            for k in range(3):
                d = shift[0, k]
                m = d // 8 + jnp.where(j + lax.rem(d, 8) >= 8, 1, 0)
                zs = lax.rem(z - m + 2 * NZ, NZ)
                got = zb[ch][zs, jnp.where(z - m >= 0, 0, 1)]
                for half in range(2):
                    sel[ch][half, k * 2 * CR : (k + 1) * 2 * CR] = got[half * 2 * CR : (half + 1) * 2 * CR]
            send(ch, 0, sel[ch], tw[ch], twin)
        if step == 1:
            arrive(ch, 0, tw[ch], twin)
            for k in range(3):
                rho, swap = turn(k)
                rows = slice(k * 2 * CR, (k + 1) * 2 * CR)
                for half in range(2):
                    my[ch][half, rows] = jnp.where(swap, tw[ch][half, rows], sel[ch][half, rows])
                msg_l[ch][rows] = jnp.where(rho == 2, my[ch][1, rows], my[ch][0, rows])
            send(ch, 1, my[ch].at[0], a_l[ch], right)
            send(ch, 2, msg_l[ch], a_r[ch], left)
        if step == 2:
            arrive(ch, 1, a_l[ch], right)
            arrive(ch, 2, a_r[ch], left)
            for k in range(3):
                rho, _ = turn(k)
                rows = slice(k * 2 * CR, (k + 1) * 2 * CR)
                fwd_r[ch][rows] = jnp.where(rho == 2, a_l[ch][rows], my[ch][1, rows])
                fwd_l[ch][rows] = jnp.where(rho == 2, a_r[ch][rows], my[ch][1, rows])
            send(ch, 3, fwd_r[ch], b_l[ch], right)
            send(ch, 4, fwd_l[ch], b_r[ch], left)
        if step == 3:
            arrive(ch, 3, b_l[ch], right)
            arrive(ch, 4, b_r[ch], left)
            for k in range(3):
                rho, _ = turn(k)
                rows = slice(k * 2 * CR, (k + 1) * 2 * CR)
                lo = ch * SK + k * 2 * CR
                kall[lo : lo + 2 * CR] = jnp.where(
                    rho == 0, my[ch][0, rows],
                    jnp.where(rho == 1, a_l[ch][rows], jnp.where(rho == 2, b_l[ch][rows], a_r[ch][rows])),
                )
                vall[lo : lo + 2 * CR, :128] = jnp.where(
                    rho == 0, my[ch][1, rows], jnp.where(rho == 1, b_l[ch][rows], b_r[ch][rows])
                )

    zc = lax.rem(z, NC)

    def pcopy(slot, view, dst, to):
        return pltpu.make_async_remote_copy(
            src_ref=view, dst_ref=dst, send_sem=psend.at[slot], recv_sem=precv.at[slot],
            device_id=to, device_id_type=MESH,
        )

    def psent(slot, view, dst, to):
        cp = pcopy(slot, view, dst, to)
        cp.start()
        started.append(cp)

    def parrive(slot, dst, to):
        pcopy(slot, dst, dst, to).wait_recv()

    def pstep(step):
        if step == 0:
            for i in range(4):
                p = pages[0, i]
                got = zb[0][p // 16, 1]
                for ch in range(1, NC):
                    got = jnp.where(zc == ch, zb[ch][p // 16, 1], got)
                for half in range(2):
                    lo = half * 2 * CR
                    psel[half, i * CR : (i + 1) * CR] = jnp.where(
                        lax.rem(p, 2) == 0, got[lo : lo + CR], got[lo + CR : lo + 2 * CR]
                    )
            psent(0, psel, ptw, twin)
        if step == 1:
            parrive(0, ptw, twin)
            for i in range(4):
                mine = lax.rem(pages[0, i] // 2, 2) == c
                rows = slice(i * CR, (i + 1) * CR)
                keys_i = jnp.where(mine, psel[0, rows], ptw[0, rows])
                vals_i = jnp.where(mine, psel[1, rows], ptw[1, rows])
                pg[rows] = jnp.where(c == 0, keys_i, vals_i)
            psent(1, pg, pa_l, right)
            psent(2, pg, pa_r, left)
        if step == 2:
            parrive(1, pa_l, right)
            parrive(2, pa_r, left)
            psent(3, pa_l.at[pl.ds(0, PK // 2)], pb_l, right)
            psent(4, pa_r.at[pl.ds(PK // 2, PK // 2)], pb_r, left)
        if step == 3:
            parrive(3, pb_l, right)
            parrive(4, pb_r, left)
            for i in range(4):
                far = lax.rem(lax.rem(pages[0, i] // 4, NX) - x + NX, NX)
                rows = slice(i * CR, (i + 1) * CR)
                opposite = (pb_l if i < 2 else pb_r)[i % 2 * CR : (i % 2 + 1) * CR]
                pcol[zc, rows] = jnp.where(
                    far == 0, pg[rows],
                    jnp.where(far == 3, pa_l[rows], jnp.where(far == 1, pa_r[rows], opposite)),
                )
            psent(5, pcol.at[zc], pcol.at[zc], up)
            psent(6, pcol.at[zc], pcol.at[zc], down)
            psent(7, pcol.at[zc], pcol.at[zc], up2)
        if step == 4:
            parrive(5, pcol.at[lax.rem(zc + 3, NC)], up)
            parrive(6, pcol.at[lax.rem(zc + 1, NC)], down)
            parrive(7, pcol.at[lax.rem(zc + 2, NC)], up2)
            psent(8, pcol, pcol2, twin)
        if step == 5:
            parrive(8, pcol2, twin)
            for ch in range(NC):
                lo = NC * SK + ch * PK
                kall[lo : lo + PK] = jnp.where(c == 0, pcol[ch], pcol2[ch])
                vall[lo : lo + PK, :128] = jnp.where(c == 0, pcol2[ch], pcol[ch])

    for hop in range(8):
        for ch in range(NC):
            zstep(ch, hop)
        if hop == 0:
            for cp in local:
                cp.start()
        if hop == 1:
            vall[:, 128:] = jnp.ones((NC * KC + NC * 2 * CR, 128), jnp.bfloat16)
            for ch in range(NC):
                lo = NC * KC + ch * 2 * CR
                kall[lo : lo + 2 * CR] = slab[ch, 0].reshape(2 * CR, 128)
                vall[lo : lo + 2 * CR, :128] = slab[ch, 1].reshape(2 * CR, 128)
        if hop == 4:
            for cp in local:
                cp.wait()
    for ch in range(NC):
        xstep(ch, 0)
    pstep(0)
    for step in (1, 2, 3):
        for ch in range(NC):
            xstep(ch, step)
            if ch == 0:
                pstep(step)
            if step == 3 and ch == 2:
                pstep(4)
    pstep(5)

    own = NC * 2 * CR
    rows_t = own // NT
    scale = 128**-0.5 * 1.4426950408889634
    lane = lax.broadcasted_iota(jnp.int32, (1, NC * KC), 1)
    bias = jnp.zeros((1, NC * KC), jnp.float32)
    for k in range(3):
        here = (lane < NC * SK) & (lane % SK // (2 * CR) == k)
        bias = jnp.where(here & (live[0, k] != 1), NEG, bias)
    for i in range(4):
        shut = False
        for k in range(3):
            d = shift[0, k]
            shut = shut | ((live[0, k] == 1) & (d > s) & (s + 128 - d == pages[0, i] // 2))
        here = (lane >= NC * SK) & ((lane - NC * SK) % PK // CR == i)
        bias = jnp.where(here & shut, NEG, bias)
    spot = lax.broadcasted_iota(jnp.int32, (rows_t, own), 1)
    cols = (spot // CR) % 2 * 128 + spot // (2 * CR) * CR + spot % CR
    line = lax.broadcasted_iota(jnp.int32, (rows_t, own), 0)

    contract = (((1,), (1,)), ((), ()))
    far = NC * KC
    own_parts = []

    def ycopy(t, step):
        lines = pl.ds(t * rows_t, rows_t)
        return pltpu.make_async_remote_copy(
            src_ref=parts.at[step - 1, lines], dst_ref=inbox.at[step - 1, lines],
            send_sem=ysend.at[t, step - 1], recv_sem=yrecv.at[t, step - 1],
            device_id=(s, lax.rem(y + step, 4)), device_id_type=MESH,
        )

    for t in range(NT):
        lines = slice(t * rows_t, (t + 1) * rows_t)
        qt = jnp.concatenate([q[lines, h * 128 : (h + 1) * 128] for h in range(8)], 0)
        s1 = lax.dot_general(qt, kall[:far], contract, preferred_element_type=jnp.float32)
        s0 = lax.dot_general(qt, kall[far:], contract, preferred_element_type=jnp.float32)
        s1 = s1 + bias
        open_ = jnp.where(line + t * rows_t >= cols, 0.0, NEG)
        s0 = s0 + jnp.concatenate([open_] * 8, 0)
        top = jnp.maximum(jnp.max(s0, 1, keepdims=True), jnp.max(s1, 1, keepdims=True))
        e0 = jnp.exp2((s0 - top) * scale)
        e1 = jnp.exp2((s1 - top) * scale)
        o = jnp.dot(e1.astype(jnp.bfloat16), vall[:far], preferred_element_type=jnp.float32)
        o += jnp.dot(e0.astype(jnp.bfloat16), vall[far:], preferred_element_type=jnp.float32)
        o = (o[:, :128] / o[:, 128:]).astype(jnp.bfloat16)
        for h in range(8):
            att[lines, h * 128 : (h + 1) * 128] = o[h * rows_t : (h + 1) * rows_t]
        a = att[lines]
        for step in (2, 1, 3, 0):
            cols_y = pl.ds(pl.multiple_of(lax.rem(y + step, 4) * 512, 512), 512)
            term = jnp.dot(a, w[:, cols_y], preferred_element_type=jnp.float32)
            if step:
                parts[step - 1, lines] = term.astype(jnp.bfloat16)
                cp = ycopy(t, step)
                cp.start()
                started.append(cp)
            else:
                own_parts.append(term)
    for t in range(NT):
        lines = slice(t * rows_t, (t + 1) * rows_t)
        total = own_parts[t]
        for step in (1, 3, 2):
            ycopy(t, step).wait_recv()
            total = total + inbox[step - 1, lines].astype(jnp.float32)
        out[lines] = total.astype(jnp.bfloat16)
    for cp in started:
        cp.wait_send()


def call(shift, pages, live, slab, cache, q, w):
    smem = pl.BlockSpec(memory_space=pltpu.SMEM)
    vmem = pl.BlockSpec(memory_space=pltpu.VMEM)
    whole = pl.BlockSpec(memory_space=pl.ANY)
    bf, dma = jnp.bfloat16, pltpu.SemaphoreType.DMA
    rows = q.shape[0]
    keys = NC * KC + NC * 2 * CR

    def many(*shape):
        return [pltpu.VMEM(shape, bf)] * NC

    return pl.pallas_call(
        kernel,
        name="attention",
        out_shape=jax.ShapeDtypeStruct((rows, 512), bf),
        in_specs=[smem, smem, smem, vmem, vmem, whole, whole],
        out_specs=vmem,
        scratch_shapes=many(NZ, 2, 4 * CR, 128)
        + many(2, SK, 128) * 3
        + many(SK, 128) * 7
        + [pltpu.VMEM((2, PK, 128), bf)] * 2
        + [pltpu.VMEM((PK, 128), bf)] * 3
        + [pltpu.VMEM((PK // 2, 128), bf)] * 2
        + [pltpu.VMEM((NC, PK, 128), bf)] * 2
        + [
            pltpu.VMEM(q.shape, bf),
            pltpu.VMEM(w.shape, bf),
            pltpu.VMEM((keys, 128), bf),
            pltpu.VMEM((keys, 256), bf),
            pltpu.VMEM(q.shape, bf),
            pltpu.VMEM((3, rows, 512), bf),
            pltpu.VMEM((3, rows, 512), bf),
        ]
        + [dma((NC, 2, 8))] * 2 + [dma((NC, 5))] * 2 + [dma((9,))] * 2 + [dma((NT, 3))] * 2 + [dma((2,))],
        compiler_params=pltpu.CompilerParams(
            collective_id=0, has_side_effects=True, vmem_limit_bytes=56 * 2**20
        ),
    )(shift, pages, live, slab, cache, q, w)


def chunked(kv):
    return kv.reshape(2, NC, CR, 2, 128).transpose(1, 3, 0, 2, 4)


def body(queries, keys_values, cache_kv, vertical_pages, slash_shift, slash_live, out_proj):
    return call(
        slash_shift, vertical_pages, slash_live[0], chunked(keys_values), chunked(cache_kv), queries, out_proj
    )


def solution(mesh):
    placed = (
        P("seq", "head"),
        P("seq", None, "head"),
        P("seq", None, "head"),
        P("head", None),
        P("head", None),
        P("seq", "head", None),
        P("head", None),
    )
    return jax.shard_map(
        body, mesh=mesh, in_specs=placed, out_specs=P("seq", "head"), check_vma=False
    )
```

time: 559 us -> 97.2 us (0.17)
  waiting for transfers between devices: 413 us -> 0 us
  Pallas kernels: 0 us -> 93.6 us
  starting transfers between devices: 86.4 us -> 0 us
  between operations: 30.4 us -> 0.01 us
  matrix products: 15.3 us -> 0 us
  other arithmetic: 8.8 us -> 0 us
    psum x1 -> x0, waiting for transfers between devices: 319 us -> none  [broadcast(): return lax.psum(kept, axis)]
    pallas_call x0 -> x1, Pallas kernels: none -> 93.6 us  [call(): pl.pallas_call(kernel, name='attention', out_shape=jax.ShapeDtypeStruct((...]
    ppermute x21 -> x0, starting transfers between devices: 86.4 us -> none  [passed_along(): return lax.ppermute(value, axis, pairs)]
    reduce_scatter x1 -> x0, waiting for transfers between devices: 72.3 us -> none  [body(): lax.psum_scatter(group_terms, 'head', scatter_dimension=1, tiled=True)]
    ppermute x21 -> x0, waiting for transfers between devices: 21.6 us -> none  [passed_along(): return lax.ppermute(value, axis, pairs)]
    dot_general x2 -> x0, matrix products: 8.35 us -> none  [the longest x1 5.73 us: body(): jnp.einsum('grk,kd->rgd', weights_bf, all_keys[:, 1, :], preferred_elemen...]
    sub x1 -> x0, matrix products: 6.91 us -> none  [body(): weights = jnp.exp(scores - row_max)]
  transfers between devices with their start and end apart: 23 -> 0, of which waited for: 5 -> 0; matrix products, arithmetic and copies ran while one was open for 2% -> 0% of each run, Pallas kernels for 0% -> 0%
where the time goes in v2:
time: 97.2 us; the launch traced here: 97 us
  Pallas kernels  93.6 us (96%)
  local copies, waits for them, and re-layouts  3.39 us (3%)
    pallas_call x1, Pallas kernels, call(): pl.pallas_call(kernel, name='attention', out_shape=jax.ShapeDtypeStruct((...  93.6 us

profile of v2, /device:TPU:1, one launch (start us, length us, event | category | flops | bytes accessed | tf_op | source)
XLA Modules:
  0.0 97.0 jit_solution(16556130633013458800)
XLA Ops:
  0.0 1.7 %copy_bitcast_fusion = (bf16[4,2,2,32,128]{4,3,2,1,0:T(8,128)(2,1)}, bf16[4,2,2,32,128]{4,3,2,1,0:T(8,128)(2,1)}) fusion(bf16[2,4,32,2,128]{4,3,2,1,0:T(2,128)(2,1)} %bitcast.7, bf16[2,4,32,2,128]{4,3,2,1,0:T(2,128)(2,1)} %bitcast.8), kind=kLoop, calls=%fused_computation | loop fusion | bytes 524288 | tf_op jit(solution)/shard_map/transpose | solution.py:358
  1.7 93.6 %attention.1 = bf16[256,512]{1,0:T(8,128)(2,1)} custom-call(s32[1,3]{1,0:T(1,128)} %shift.1, s32[1,4]{1,0:T(1,128)} %pages.1, s32[1,3]{1,0:T(1,128)} %bitcast.9, bf16[4,2,2,32,128]{4,3,2,1,0:T(8,128)(2,1)} %get-tuple-element.6.slab, bf16[4,2,2,32,128]{4,3,2,1,0:T(8,128)(2,1)} %get-tuple-element.5.cache, bf16[256,1024]{1,0:T(8,128)(2,1)} %q_hbm.1, ...), custom_call_target="tpu_custom_call" | custom-call | tf_op jit(solution)/shard_map/attention/pallas_call | solution.py:328
  95.4 1.7 %copy.19 = bf16[256,512]{1,0:T(8,128)(2,1)} copy(bf16[256,512]{1,0:T(8,128)(2,1)} %attention.1) | data formatting | bytes 524288

commit v3 on v2

--- a/solution.py
+++ b/solution.py
@@ -10,7 +10,8 @@
 MESH = pl.DeviceIdType.MESH
 NC = 4
 NZ, NX = 16, 4
-NT = 4
+TILES = (96, 96, 64)
+NT = len(TILES)
 CR = 32
 KC = 3 * 2 * CR + 4 * CR
 NEG = -1e30
@@ -35,7 +36,8 @@
         scratch[NC * (i + 1) : NC * (i + 2)] for i in range(10)
     )
     (psel, ptw, pg, pa_l, pa_r, pb_l, pb_r, pcol, pcol2,
-     q, w, kall, vall, att, parts, inbox,
+     q, w, qs, kall, vall, att, near, t0, t1, t3,
+     p2a, p2b, s1a, s1b, s3a, s3b, hop_l, hop_r, in_la, in_lb, in_ra, in_rb,
      zsend, zrecv, xsend, xrecv, psend, precv, ysend, yrecv, lsem) = scratch[11 * NC :]
     s = lax.axis_index("seq")
     z, x, c, y = place()
@@ -45,7 +47,7 @@
     twin = at(z, x, 1 - c, y)
 
     bar = pltpu.get_barrier_semaphore()
-    others = [(s, lax.rem(y + step, 4)) for step in (1, 2, 3)]
+    others = [(s, lax.rem(y + step, 4)) for step in (1, 3)]
     up2, down2 = at(z + 2, x, c, y), at(z - 2, x, c, y)
     for peer in [up, down, down2, right, left, twin] + others:
         pl.semaphore_signal(bar, inc=1, device_id=peer, device_id_type=MESH)
@@ -56,7 +58,7 @@
     for ch in range(NC):
         zb[ch][z, 0] = slab[ch].reshape(4 * CR, 128)
         zb[ch][z, 1] = cache[ch].reshape(4 * CR, 128)
-    pl.semaphore_wait(bar, 9)
+    pl.semaphore_wait(bar, 8)
 
     started = []
 
@@ -206,21 +208,58 @@
             psent(5, pcol.at[zc], pcol.at[zc], up)
             psent(6, pcol.at[zc], pcol.at[zc], down)
             psent(7, pcol.at[zc], pcol.at[zc], up2)
+            psent(8, pcol.at[zc], pcol2.at[zc], twin)
         if step == 4:
-            parrive(5, pcol.at[lax.rem(zc + 3, NC)], up)
-            parrive(6, pcol.at[lax.rem(zc + 1, NC)], down)
-            parrive(7, pcol.at[lax.rem(zc + 2, NC)], up2)
-            psent(8, pcol, pcol2, twin)
+            for slot, to, far in ((5, up, 3), (6, down, 1), (7, up2, 2)):
+                row = lax.rem(zc + far, NC)
+                parrive(slot, pcol.at[row], to)
+                psent(slot + 4, pcol.at[row], pcol2.at[row], twin)
         if step == 5:
-            parrive(8, pcol2, twin)
+            for slot, far in ((8, 0), (9, 3), (10, 1), (11, 2)):
+                parrive(slot, pcol2.at[lax.rem(zc + far, NC)], twin)
             for ch in range(NC):
                 lo = NC * SK + ch * PK
                 kall[lo : lo + PK] = jnp.where(c == 0, pcol[ch], pcol2[ch])
                 vall[lo : lo + PK, :128] = jnp.where(c == 0, pcol2[ch], pcol[ch])
 
+    own = NC * 2 * CR
+    scale = 128**-0.5 * 1.4426950408889634
+    contract = (((1,), (1,)), ((), ()))
+    far = NC * KC
+    first = [sum(TILES[:t]) for t in range(NT)]
+
+    def spans(t):
+        lo, hi = first[t], first[t] + TILES[t]
+        return slice(lo, hi), slice(8 * lo, 8 * hi)
+
+    def own_block(t):
+        lines, block = spans(t)
+        qs[block] = jnp.concatenate([q[lines, h * 128 : (h + 1) * 128] for h in range(8)], 0)
+        spot = lax.broadcasted_iota(jnp.int32, (TILES[t], own), 1)
+        cols = (spot // CR) % 2 * 128 + spot // (2 * CR) * CR + spot % CR
+        line = lax.broadcasted_iota(jnp.int32, (TILES[t], own), 0) + first[t]
+        shade = jnp.concatenate([jnp.where(line >= cols, 0.0, NEG)] * 8, 0)
+        near[block] = shade + lax.dot_general(
+            qs[block], kall[far:], contract, preferred_element_type=jnp.float32
+        )
+
+    lane = lax.broadcasted_iota(jnp.int32, (1, NC * KC), 1)
+    bias = jnp.zeros((1, NC * KC), jnp.float32)
+    for k in range(3):
+        here = (lane < NC * SK) & (lane % SK // (2 * CR) == k)
+        bias = jnp.where(here & (live[0, k] != 1), NEG, bias)
+    for i in range(4):
+        shut = False
+        for k in range(3):
+            d = shift[0, k]
+            shut = shut | ((live[0, k] == 1) & (d > s) & (s + 128 - d == pages[0, i] // 2))
+        here = (lane >= NC * SK) & ((lane - NC * SK) % PK // CR == i)
+        bias = jnp.where(here & shut, NEG, bias)
     for hop in range(8):
         for ch in range(NC):
             zstep(ch, hop)
+            if hop >= 5 and (hop - 5) * NC + ch < NT:
+                own_block((hop - 5) * NC + ch)
         if hop == 0:
             for cp in local:
                 cp.start()
@@ -235,81 +274,80 @@
                 cp.wait()
     for ch in range(NC):
         xstep(ch, 0)
-    pstep(0)
-    for step in (1, 2, 3):
-        for ch in range(NC):
-            xstep(ch, step)
-            if ch == 0:
-                pstep(step)
-            if step == 3 and ch == 2:
-                pstep(4)
-    pstep(5)
-
-    own = NC * 2 * CR
-    rows_t = own // NT
-    scale = 128**-0.5 * 1.4426950408889634
-    lane = lax.broadcasted_iota(jnp.int32, (1, NC * KC), 1)
-    bias = jnp.zeros((1, NC * KC), jnp.float32)
-    for k in range(3):
-        here = (lane < NC * SK) & (lane % SK // (2 * CR) == k)
-        bias = jnp.where(here & (live[0, k] != 1), NEG, bias)
-    for i in range(4):
-        shut = False
-        for k in range(3):
-            d = shift[0, k]
-            shut = shut | ((live[0, k] == 1) & (d > s) & (s + 128 - d == pages[0, i] // 2))
-        here = (lane >= NC * SK) & ((lane - NC * SK) % PK // CR == i)
-        bias = jnp.where(here & shut, NEG, bias)
-    spot = lax.broadcasted_iota(jnp.int32, (rows_t, own), 1)
-    cols = (spot // CR) % 2 * 128 + spot // (2 * CR) * CR + spot % CR
-    line = lax.broadcasted_iota(jnp.int32, (rows_t, own), 0)
-
-    contract = (((1,), (1,)), ((), ()))
-    far = NC * KC
-    own_parts = []
-
-    def ycopy(t, step):
-        lines = pl.ds(t * rows_t, rows_t)
+    for page, *moves in (
+        (0,), (1, (0, 1), (1, 1), (2, 1), (3, 1)), (2, (0, 2), (1, 2)), (3, (2, 2), (3, 2), (0, 3)),
+        (4, (1, 3), (2, 3)), (5, (3, 3)),
+    ):
+        pstep(page)
+        for move in moves:
+            xstep(*move)
+
+    def ycopy(t, slot):
+        lines = pl.ds(first[t], TILES[t])
+        view, dst, step = (
+            (p2a, hop_l, 1), (p2b, hop_r, 3), (s1b, in_lb, 1), (s3a, in_ra, 3), (s1a, in_la, 1), (s3b, in_rb, 3),
+        )[slot]
         return pltpu.make_async_remote_copy(
-            src_ref=parts.at[step - 1, lines], dst_ref=inbox.at[step - 1, lines],
-            send_sem=ysend.at[t, step - 1], recv_sem=yrecv.at[t, step - 1],
+            src_ref=view.at[lines], dst_ref=dst.at[lines],
+            send_sem=ysend.at[t, slot], recv_sem=yrecv.at[t, slot],
             device_id=(s, lax.rem(y + step, 4)), device_id_type=MESH,
         )
 
+    def ysent(t, slot):
+        cp = ycopy(t, slot)
+        cp.start()
+        started.append(cp)
+
+    def relay(t):
+        lines, _ = spans(t)
+        ycopy(t, 0).wait_recv()
+        s1a[lines] = (t1[lines] + hop_l[lines].astype(jnp.float32)).astype(jnp.bfloat16)
+        ysent(t, 4)
+        ycopy(t, 1).wait_recv()
+        s3b[lines] = (t3[lines] + hop_r[lines].astype(jnp.float32)).astype(jnp.bfloat16)
+        ysent(t, 5)
+
     for t in range(NT):
-        lines = slice(t * rows_t, (t + 1) * rows_t)
-        qt = jnp.concatenate([q[lines, h * 128 : (h + 1) * 128] for h in range(8)], 0)
-        s1 = lax.dot_general(qt, kall[:far], contract, preferred_element_type=jnp.float32)
-        s0 = lax.dot_general(qt, kall[far:], contract, preferred_element_type=jnp.float32)
+        lines, block = spans(t)
+        s1 = lax.dot_general(qs[block], kall[:far], contract, preferred_element_type=jnp.float32)
         s1 = s1 + bias
-        open_ = jnp.where(line + t * rows_t >= cols, 0.0, NEG)
-        s0 = s0 + jnp.concatenate([open_] * 8, 0)
+        s0 = near[block]
         top = jnp.maximum(jnp.max(s0, 1, keepdims=True), jnp.max(s1, 1, keepdims=True))
-        e0 = jnp.exp2((s0 - top) * scale)
-        e1 = jnp.exp2((s1 - top) * scale)
-        o = jnp.dot(e1.astype(jnp.bfloat16), vall[:far], preferred_element_type=jnp.float32)
-        o += jnp.dot(e0.astype(jnp.bfloat16), vall[far:], preferred_element_type=jnp.float32)
+        e0 = jnp.exp2((s0 - top) * scale).astype(jnp.bfloat16)
+        e1 = jnp.exp2((s1 - top) * scale).astype(jnp.bfloat16)
+        o = jnp.dot(e1, vall[:far], preferred_element_type=jnp.float32)
+        o += jnp.dot(e0, vall[far:], preferred_element_type=jnp.float32)
         o = (o[:, :128] / o[:, 128:]).astype(jnp.bfloat16)
         for h in range(8):
-            att[lines, h * 128 : (h + 1) * 128] = o[h * rows_t : (h + 1) * rows_t]
+            att[lines, h * 128 : (h + 1) * 128] = o[h * TILES[t] : (h + 1) * TILES[t]]
         a = att[lines]
-        for step in (2, 1, 3, 0):
+
+        def term(step):
             cols_y = pl.ds(pl.multiple_of(lax.rem(y + step, 4) * 512, 512), 512)
-            term = jnp.dot(a, w[:, cols_y], preferred_element_type=jnp.float32)
-            if step:
-                parts[step - 1, lines] = term.astype(jnp.bfloat16)
-                cp = ycopy(t, step)
-                cp.start()
-                started.append(cp)
-            else:
-                own_parts.append(term)
+            return jnp.dot(a, w[:, cols_y], preferred_element_type=jnp.float32)
+
+        both = term(2).astype(jnp.bfloat16)
+        p2a[lines], p2b[lines] = both[:, :256], both[:, 256:]
+        ysent(t, 0)
+        ysent(t, 1)
+        if t:
+            relay(t - 1)
+        side = term(1)
+        t1[lines], s1b[lines] = side[:, :256], side[:, 256:].astype(jnp.bfloat16)
+        ysent(t, 2)
+        side = term(3)
+        s3a[lines], t3[lines] = side[:, :256].astype(jnp.bfloat16), side[:, 256:]
+        ysent(t, 3)
+        t0[lines] = term(0)
+    relay(NT - 1)
     for t in range(NT):
-        lines = slice(t * rows_t, (t + 1) * rows_t)
-        total = own_parts[t]
-        for step in (1, 3, 2):
-            ycopy(t, step).wait_recv()
-            total = total + inbox[step - 1, lines].astype(jnp.float32)
-        out[lines] = total.astype(jnp.bfloat16)
+        lines, _ = spans(t)
+        for slot in (2, 3, 4, 5):
+            ycopy(t, slot).wait_recv()
+        for half, ins in ((slice(0, 256), (in_la, in_ra)), (slice(256, 512), (in_lb, in_rb))):
+            out[lines, half] = (
+                t0[lines, half] + ins[0][lines].astype(jnp.float32) + ins[1][lines].astype(jnp.float32)
+            ).astype(jnp.bfloat16)
     for cp in started:
         cp.wait_send()
 
@@ -341,13 +379,17 @@
         + [
             pltpu.VMEM(q.shape, bf),
             pltpu.VMEM(w.shape, bf),
+            pltpu.VMEM((8 * rows, 128), bf),
             pltpu.VMEM((keys, 128), bf),
             pltpu.VMEM((keys, 256), bf),
             pltpu.VMEM(q.shape, bf),
-            pltpu.VMEM((3, rows, 512), bf),
-            pltpu.VMEM((3, rows, 512), bf),
+            pltpu.VMEM((8 * rows, NC * 2 * CR), jnp.float32),
+            pltpu.VMEM((rows, 512), jnp.float32),
+            pltpu.VMEM((rows, 256), jnp.float32),
+            pltpu.VMEM((rows, 256), jnp.float32),
         ]
-        + [dma((NC, 2, 8))] * 2 + [dma((NC, 5))] * 2 + [dma((9,))] * 2 + [dma((NT, 3))] * 2 + [dma((2,))],
+        + [pltpu.VMEM((rows, 256), bf)] * 12
+        + [dma((NC, 2, 8))] * 2 + [dma((NC, 5))] * 2 + [dma((12,))] * 2 + [dma((NT, 6))] * 2 + [dma((2,))],
         compiler_params=pltpu.CompilerParams(
             collective_id=0, has_side_effects=True, vmem_limit_bytes=56 * 2**20
         ),

time: 97.2 us -> 95 us (0.977)
  Pallas kernels: 93.6 us -> 91.2 us
    pallas_call x1, Pallas kernels: 93.6 us -> 91.2 us  [call(): pl.pallas_call(kernel, name='attention', out_shape=jax.ShapeDtypeStruct((...]
where the time goes in v3:
time: 95 us; the launch traced here: 94.6 us
  Pallas kernels  91.2 us (96%)
  local copies, waits for them, and re-layouts  3.39 us (4%)
    pallas_call x1, Pallas kernels, call(): pl.pallas_call(kernel, name='attention', out_shape=jax.ShapeDtypeStruct((...  91.2 us

profile of v3, /device:TPU:1, one launch (start us, length us, event | category | flops | bytes accessed | tf_op | source)
XLA Modules:
  0.0 94.6 jit_solution(11105568527709931538)
XLA Ops:
  0.0 1.7 %copy_bitcast_fusion = (bf16[4,2,2,32,128]{4,3,2,1,0:T(8,128)(2,1)}, bf16[4,2,2,32,128]{4,3,2,1,0:T(8,128)(2,1)}) fusion(bf16[2,4,32,2,128]{4,3,2,1,0:T(2,128)(2,1)} %bitcast.7, bf16[2,4,32,2,128]{4,3,2,1,0:T(2,128)(2,1)} %bitcast.8), kind=kLoop, calls=%fused_computation | loop fusion | bytes 524288 | tf_op jit(solution)/shard_map/transpose | solution.py:400
  1.7 91.2 %attention.1 = bf16[256,512]{1,0:T(8,128)(2,1)} custom-call(s32[1,3]{1,0:T(1,128)} %shift.1, s32[1,4]{1,0:T(1,128)} %pages.1, s32[1,3]{1,0:T(1,128)} %bitcast.9, bf16[4,2,2,32,128]{4,3,2,1,0:T(8,128)(2,1)} %get-tuple-element.6.slab, bf16[4,2,2,32,128]{4,3,2,1,0:T(8,128)(2,1)} %get-tuple-element.5.cache, bf16[256,1024]{1,0:T(8,128)(2,1)} %q_hbm.1, ...), custom_call_target="tpu_custom_call" | custom-call | tf_op jit(solution)/shard_map/attention/pallas_call | solution.py:366
  93.0 1.7 %copy.19 = bf16[256,512]{1,0:T(8,128)(2,1)} copy(bf16[256,512]{1,0:T(8,128)(2,1)} %attention.1) | data formatting | bytes 524288

commit v4 on v3

--- a/solution.py
+++ b/solution.py
@@ -35,7 +35,7 @@
     sel, tw, my, msg_l, fwd_r, fwd_l, a_l, a_r, b_l, b_r = (
         scratch[NC * (i + 1) : NC * (i + 2)] for i in range(10)
     )
-    (psel, ptw, pg, pa_l, pa_r, pb_l, pb_r, pcol, pcol2,
+    (psel, ptw, pg, pa_l, pa_r, pa_o, pcol, pcol2,
      q, w, qs, kall, vall, att, near, t0, t1, t3,
      p2a, p2b, s1a, s1b, s3a, s3b, hop_l, hop_r, in_la, in_lb, in_ra, in_rb,
      zsend, zrecv, xsend, xrecv, psend, precv, ysend, yrecv, lsem) = scratch[11 * NC :]
@@ -49,7 +49,8 @@
     bar = pltpu.get_barrier_semaphore()
     others = [(s, lax.rem(y + step, 4)) for step in (1, 3)]
     up2, down2 = at(z + 2, x, c, y), at(z - 2, x, c, y)
-    for peer in [up, down, down2, right, left, twin] + others:
+    across = at(z, x + 2, c, y)
+    for peer in [up, down, down2, right, left, across, twin] + others:
         pl.semaphore_signal(bar, inc=1, device_id=peer, device_id_type=MESH)
     local = [
         pltpu.make_async_copy(q_hbm, q, lsem.at[0]),
@@ -58,7 +59,7 @@
     for ch in range(NC):
         zb[ch][z, 0] = slab[ch].reshape(4 * CR, 128)
         zb[ch][z, 1] = cache[ch].reshape(4 * CR, 128)
-    pl.semaphore_wait(bar, 8)
+    pl.semaphore_wait(bar, 9)
 
     started = []
 
@@ -105,8 +106,6 @@
 
     def xstep(ch, step):
         if step == 0:
-            for way in range(2):
-                zarrive(ch, way, 7)
             for k in range(3):
                 d = shift[0, k]
                 m = d // 8 + jnp.where(j + lax.rem(d, 8) >= 8, 1, 0)
@@ -189,32 +188,28 @@
                 pg[rows] = jnp.where(c == 0, keys_i, vals_i)
             psent(1, pg, pa_l, right)
             psent(2, pg, pa_r, left)
+            psent(3, pg, pa_o, across)
         if step == 2:
             parrive(1, pa_l, right)
             parrive(2, pa_r, left)
-            psent(3, pa_l.at[pl.ds(0, PK // 2)], pb_l, right)
-            psent(4, pa_r.at[pl.ds(PK // 2, PK // 2)], pb_r, left)
-        if step == 3:
-            parrive(3, pb_l, right)
-            parrive(4, pb_r, left)
+            parrive(3, pa_o, across)
             for i in range(4):
                 far = lax.rem(lax.rem(pages[0, i] // 4, NX) - x + NX, NX)
                 rows = slice(i * CR, (i + 1) * CR)
-                opposite = (pb_l if i < 2 else pb_r)[i % 2 * CR : (i % 2 + 1) * CR]
                 pcol[zc, rows] = jnp.where(
                     far == 0, pg[rows],
-                    jnp.where(far == 3, pa_l[rows], jnp.where(far == 1, pa_r[rows], opposite)),
+                    jnp.where(far == 3, pa_l[rows], jnp.where(far == 1, pa_r[rows], pa_o[rows])),
                 )
             psent(5, pcol.at[zc], pcol.at[zc], up)
             psent(6, pcol.at[zc], pcol.at[zc], down)
             psent(7, pcol.at[zc], pcol.at[zc], up2)
             psent(8, pcol.at[zc], pcol2.at[zc], twin)
-        if step == 4:
+        if step == 3:
             for slot, to, far in ((5, up, 3), (6, down, 1), (7, up2, 2)):
                 row = lax.rem(zc + far, NC)
                 parrive(slot, pcol.at[row], to)
                 psent(slot + 4, pcol.at[row], pcol2.at[row], twin)
-        if step == 5:
+        if step == 4:
             for slot, far in ((8, 0), (9, 3), (10, 1), (11, 2)):
                 parrive(slot, pcol2.at[lax.rem(zc + far, NC)], twin)
             for ch in range(NC):
@@ -273,10 +268,11 @@
             for cp in local:
                 cp.wait()
     for ch in range(NC):
-        xstep(ch, 0)
+        for way in range(2):
+            zarrive(ch, way, 7)
     for page, *moves in (
-        (0,), (1, (0, 1), (1, 1), (2, 1), (3, 1)), (2, (0, 2), (1, 2)), (3, (2, 2), (3, 2), (0, 3)),
-        (4, (1, 3), (2, 3)), (5, (3, 3)),
+        (0, (0, 0), (1, 0), (2, 0), (3, 0)), (1, (0, 1), (1, 1), (2, 1), (3, 1), (0, 2)),
+        (2, (1, 2), (2, 2), (3, 2)), (3, (0, 3), (1, 3), (2, 3)), (4, (3, 3)),
     ):
         pstep(page)
         for move in moves:
@@ -373,8 +369,7 @@
         + many(2, SK, 128) * 3
         + many(SK, 128) * 7
         + [pltpu.VMEM((2, PK, 128), bf)] * 2
-        + [pltpu.VMEM((PK, 128), bf)] * 3
-        + [pltpu.VMEM((PK // 2, 128), bf)] * 2
+        + [pltpu.VMEM((PK, 128), bf)] * 4
         + [pltpu.VMEM((NC, PK, 128), bf)] * 2
         + [
             pltpu.VMEM(q.shape, bf),

time: 95 us -> 94.5 us (level)
  no operation moved by 1% of the time
where the time goes in v4:
time: 94.5 us; the launch traced here: 94.3 us
  Pallas kernels  90.9 us (96%)
  local copies, waits for them, and re-layouts  3.39 us (4%)
    pallas_call x1, Pallas kernels, call(): pl.pallas_call(kernel, name='attention', out_shape=jax.ShapeDtypeStruct((...  90.9 us

profile of v4, /device:TPU:1, one launch (start us, length us, event | category | flops | bytes accessed | tf_op | source)
XLA Modules:
  0.0 94.3 jit_solution(11434329060950397304)
XLA Ops:
  0.0 1.7 %copy_bitcast_fusion = (bf16[4,2,2,32,128]{4,3,2,1,0:T(8,128)(2,1)}, bf16[4,2,2,32,128]{4,3,2,1,0:T(8,128)(2,1)}) fusion(bf16[2,4,32,2,128]{4,3,2,1,0:T(2,128)(2,1)} %bitcast.7, bf16[2,4,32,2,128]{4,3,2,1,0:T(2,128)(2,1)} %bitcast.8), kind=kLoop, calls=%fused_computation | loop fusion | bytes 524288 | tf_op jit(solution)/shard_map/transpose | solution.py:395
  1.7 90.9 %attention.1 = bf16[256,512]{1,0:T(8,128)(2,1)} custom-call(s32[1,3]{1,0:T(1,128)} %shift.1, s32[1,4]{1,0:T(1,128)} %pages.1, s32[1,3]{1,0:T(1,128)} %bitcast.9, bf16[4,2,2,32,128]{4,3,2,1,0:T(8,128)(2,1)} %get-tuple-element.6.slab, bf16[4,2,2,32,128]{4,3,2,1,0:T(8,128)(2,1)} %get-tuple-element.5.cache, bf16[256,1024]{1,0:T(8,128)(2,1)} %q_hbm.1, ...), custom_call_target="tpu_custom_call" | custom-call | tf_op jit(solution)/shard_map/attention/pallas_call | solution.py:362
  92.6 1.7 %copy.19 = bf16[256,512]{1,0:T(8,128)(2,1)} copy(bf16[256,512]{1,0:T(8,128)(2,1)} %attention.1) | data formatting | bytes 524288

commit v5 on v4

--- a/solution.py
+++ b/solution.py
@@ -10,7 +10,7 @@
 MESH = pl.DeviceIdType.MESH
 NC = 4
 NZ, NX = 16, 4
-TILES = (96, 96, 64)
+TILES = (112, 96, 48)
 NT = len(TILES)
 CR = 32
 KC = 3 * 2 * CR + 4 * CR
@@ -335,9 +335,10 @@
         s3a[lines], t3[lines] = side[:, :256].astype(jnp.bfloat16), side[:, 256:]
         ysent(t, 3)
         t0[lines] = term(0)
-    relay(NT - 1)
     for t in range(NT):
         lines, _ = spans(t)
+        if t == 1:
+            relay(NT - 1)
         for slot in (2, 3, 4, 5):
             ycopy(t, slot).wait_recv()
         for half, ins in ((slice(0, 256), (in_la, in_ra)), (slice(256, 512), (in_lb, in_rb))):

time: 94.5 us -> 94.4 us (level)
  no operation moved by 1% of the time
where the time goes in v5:
time: 94.4 us; the launch traced here: 94.3 us
  Pallas kernels  90.9 us (96%)
  local copies, waits for them, and re-layouts  3.39 us (4%)
    pallas_call x1, Pallas kernels, call(): pl.pallas_call(kernel, name='attention', out_shape=jax.ShapeDtypeStruct((...  90.9 us

profile of v5, /device:TPU:1, one launch (start us, length us, event | category | flops | bytes accessed | tf_op | source)
XLA Modules:
  0.0 94.3 jit_solution(10308574834804345021)
XLA Ops:
  0.0 1.7 %copy_bitcast_fusion = (bf16[4,2,2,32,128]{4,3,2,1,0:T(8,128)(2,1)}, bf16[4,2,2,32,128]{4,3,2,1,0:T(8,128)(2,1)}) fusion(bf16[2,4,32,2,128]{4,3,2,1,0:T(2,128)(2,1)} %bitcast.7, bf16[2,4,32,2,128]{4,3,2,1,0:T(2,128)(2,1)} %bitcast.8), kind=kLoop, calls=%fused_computation | loop fusion | bytes 524288 | tf_op jit(solution)/shard_map/transpose | solution.py:396
  1.7 90.9 %attention.1 = bf16[256,512]{1,0:T(8,128)(2,1)} custom-call(s32[1,3]{1,0:T(1,128)} %shift.1, s32[1,4]{1,0:T(1,128)} %pages.1, s32[1,3]{1,0:T(1,128)} %bitcast.9, bf16[4,2,2,32,128]{4,3,2,1,0:T(8,128)(2,1)} %get-tuple-element.6.slab, bf16[4,2,2,32,128]{4,3,2,1,0:T(8,128)(2,1)} %get-tuple-element.5.cache, bf16[256,1024]{1,0:T(8,128)(2,1)} %q_hbm.1, ...), custom_call_target="tpu_custom_call" | custom-call | tf_op jit(solution)/shard_map/attention/pallas_call | solution.py:363
  92.6 1.7 %copy.19 = bf16[256,512]{1,0:T(8,128)(2,1)} copy(bf16[256,512]{1,0:T(8,128)(2,1)} %attention.1) | data formatting | bytes 524288
